TPU v7x, 32 devices: a whole 2x2x4 slice. The times are simulated.
32 devices in a mesh: group: 2 (over y), node: 4 (over x, core), tp: 4 (over z).
Axes of the slice: x: 2, y: 2, z: 4, core: 2. Of those that a mesh axis runs over, the one named last changes fastest.
Arguments:
- hidden_in: bfloat16 [64, 3072], P(('group', 'node', 'tp')), parts along dimension 0, may hold values from -6 to 6
- queries: bfloat16 [64, 3072], P(('group', 'node'), 'tp'), parts along dimension 0, may hold values from -8 to 8
- new_keys: bfloat16 [64, 1024], P(('group', 'node'), 'tp'), parts along dimension 0, may hold values from -6 to 6
- new_values: bfloat16 [64, 1024], P(('group', 'node'), 'tp'), parts along dimension 0, may hold values from -6 to 6
- key_cache: bfloat16 [64, 224, 1024], P(('group', 'node'), None, 'tp'), parts along dimension 0, may hold values from -6 to 6
- value_cache: bfloat16 [64, 224, 1024], P(('group', 'node'), None, 'tp'), parts along dimension 0, may hold values from -6 to 6
- lengths: int32 [64], P(('group', 'node')), parts along dimension 0, may hold values from 2 to 224, as said below
- out_weight: bfloat16 [3072, 3072], P('tp'), may hold values from -0.109375 to 0.109375
- norm_gain: float32 [3072], replicated, may hold values from 0.5 to 1.5
- router: bfloat16 [3072, 4], replicated, may hold values from -0.109375 to 0.109375
- expert_ids: int32 [64, 2], P(('group', 'node', 'tp')), parts along dimension 0, may hold values from 0 to 3, all different within a row; in each aligned block of 2 rows (0 to 1, 2 to 3, ...) at most 2 rows name the same one
- gate_weight: bfloat16 [4, 3072, 8192], P('node', None, 'tp'), may hold values from -0.109375 to 0.109375
- up_weight: bfloat16 [4, 3072, 8192], P('node', None, 'tp'), may hold values from -0.109375 to 0.109375
- down_weight: bfloat16 [4, 8192, 3072], P('node', 'tp'), may hold values from -0.0625 to 0.0625
Outputs:
- layer_out: bfloat16 [64, 3072], P(('group', 'node', 'tp')), parts along dimension 0
There are 2 independent parts, one for each index of `group`. A program takes and returns all parts, laid end to end along the dimension named above; an argument that names none is the same for every part. Nothing has to cross between parts.
Inputs may be any that keep to these rules, and one draw needn't show every extreme that they name: `expert_ids`: each row names 2 different experts; in each aligned block of 2 rows (the rows of one device) no expert is named by more than 2 rows. `lengths`: in each aligned block of 2 requests one request uses all 224 cache positions.
All inputs are finite; a program needn't handle non-finite values.
Results may differ from a plain program's by a relative error of at most 0.006.
Values may be sent and summed in bfloat16 or wider, within the bound.
A program may use at most 128 MiB of HBM per device.

v0:
```python
import math

import jax
import jax.numpy as jnp
from jax import lax
from jax.sharding import PartitionSpec as P

HD = 128


def attend_local(queries, new_keys, new_values, key_cache, value_cache, lengths):
    request_count = queries.shape[0]
    kv_local = key_cache.shape[2] // HD
    group_size = queries.shape[1] // HD // kv_local
    positions_all = key_cache.shape[1]
    scaling = 1.0 / math.sqrt(HD)
    query_heads = queries.reshape(request_count, kv_local, group_size, HD)
    key_heads = key_cache.reshape(request_count, positions_all, kv_local, HD)
    value_heads = value_cache.reshape(request_count, positions_all, kv_local, HD)
    scores = (
        jnp.einsum("rkgd,rckd->rkgc", query_heads, key_heads, preferred_element_type=jnp.float32)
        * scaling
    )
    own_key = new_keys.reshape(request_count, kv_local, HD)
    own_score = (
        jnp.einsum("rkgd,rkd->rkg", query_heads, own_key, preferred_element_type=jnp.float32)
        * scaling
    )
    positions = jnp.arange(positions_all, dtype=jnp.int32)
    usable = positions[None, :] < lengths[:, None]
    scores = jnp.where(usable[:, None, None, :], scores, -jnp.inf)
    highest = jnp.maximum(jnp.max(scores, axis=-1), own_score)
    weights = jnp.exp(scores - highest[..., None])
    own_weight = jnp.exp(own_score - highest)
    denominator = jnp.sum(weights, axis=-1) + own_weight
    probabilities = (weights / denominator[..., None]).astype(jnp.bfloat16)
    own_prob = (own_weight / denominator).astype(jnp.bfloat16)
    mixture = jnp.einsum(
        "rkgc,rckd->rkgd", probabilities, value_heads, preferred_element_type=jnp.float32
    )
    own_value = new_values.reshape(request_count, kv_local, 1, HD).astype(jnp.float32)
    mixture = mixture + own_prob.astype(jnp.float32)[..., None] * own_value
    return mixture.reshape(request_count, queries.shape[1]).astype(jnp.bfloat16)


def local(
    hidden_in,
    queries,
    new_keys,
    new_values,
    key_cache,
    value_cache,
    lengths,
    out_weight,
    norm_gain,
    router,
    expert_ids,
    gate_weight,
    up_weight,
    down_weight,
):
    row_count = hidden_in.shape[0]
    width = hidden_in.shape[1]
    attended = attend_local(queries, new_keys, new_values, key_cache, value_cache, lengths)
    partial_value = jnp.dot(attended, out_weight, preferred_element_type=jnp.float32)
    summed = lax.psum(partial_value, "tp")
    own_rows = lax.dynamic_slice_in_dim(summed, lax.axis_index("tp") * row_count, row_count, 0)
    middle = (hidden_in.astype(jnp.float32) + own_rows).astype(jnp.bfloat16)
    widened = middle.astype(jnp.float32)
    scale_rms = lax.rsqrt(jnp.mean(widened * widened, axis=-1, keepdims=True) + 1e-05)
    normed = (widened * scale_rms * norm_gain).astype(jnp.bfloat16)
    logits = jnp.dot(normed, router, preferred_element_type=jnp.float32)
    expert_count = router.shape[1]
    top_count = expert_ids.shape[1]
    chosen = expert_ids[:, :, None] == jnp.arange(expert_count, dtype=jnp.int32)[None, None, :]
    picked = jnp.sum(chosen.astype(jnp.float32) * logits[:, None, :], axis=-1)
    gate_share = jax.nn.sigmoid(picked - picked[:, ::-1])
    picks_total = row_count * top_count
    flat_hot = chosen.reshape(picks_total, expert_count).astype(jnp.int32)
    earlier = jnp.cumsum(flat_hot, axis=0) - flat_hot
    rank_in = jnp.sum(earlier * flat_hot, axis=1)
    slot_index = expert_ids.reshape(picks_total) * row_count + rank_in
    slot_hot = slot_index[:, None] == jnp.arange(expert_count * row_count, dtype=jnp.int32)[None, :]
    repeated = jnp.repeat(normed, top_count, axis=0)
    send_rows = jnp.einsum(
        "ms,md->sd", slot_hot.astype(jnp.bfloat16), repeated, preferred_element_type=jnp.float32
    )
    send_rows = send_rows.astype(jnp.bfloat16).reshape(expert_count, row_count, width)
    combine = jnp.sum(
        slot_hot.reshape(row_count, top_count, expert_count * row_count).astype(jnp.float32)
        * gate_share[:, :, None],
        axis=1,
    )
    node_count = lax.axis_size("node")
    tp_count = lax.axis_size("tp")
    split_count = node_count // expert_count
    outgoing = jnp.repeat(send_rows, split_count * tp_count, axis=0)
    rows_in = lax.all_to_all(outgoing, ("node", "tp"), split_axis=0, concat_axis=0, tiled=True)
    out_shape = rows_in.shape
    flattened = rows_in.reshape(-1, out_shape[-1])
    gate_val = jnp.dot(flattened, gate_weight[0], preferred_element_type=jnp.float32)
    up_val = jnp.dot(flattened, up_weight[0], preferred_element_type=jnp.float32)
    hidden_units = (jax.nn.silu(gate_val) * up_val).astype(jnp.bfloat16)
    result = jnp.dot(hidden_units, down_weight[0], preferred_element_type=jnp.float32)
    shares = result.reshape(out_shape[:-1] + (result.shape[-1],))
    returned = lax.all_to_all(shares, ("node", "tp"), split_axis=0, concat_axis=0, tiled=True)
    per_expert = jnp.sum(
        returned.reshape(expert_count, split_count * tp_count, row_count, width), axis=1
    )
    routed = jnp.dot(
        combine,
        per_expert.reshape(expert_count * row_count, width),
        precision=lax.Precision.HIGHEST,
        preferred_element_type=jnp.float32,
    )
    return (widened + routed).astype(jnp.bfloat16)


def solution(mesh):
    placed = (
        P(("group", "node", "tp"), None),
        P(("group", "node"), "tp"),
        P(("group", "node"), "tp"),
        P(("group", "node"), "tp"),
        P(("group", "node"), None, "tp"),
        P(("group", "node"), None, "tp"),
        P(("group", "node")),
        P("tp", None),
        P(),
        P(),
        P(("group", "node", "tp"), None),
        P("node", None, "tp"),
        P("node", None, "tp"),
        P("node", "tp", None),
    )
    return jax.shard_map(
        local,
        mesh=mesh,
        in_specs=placed,
        out_specs=P(("group", "node", "tp"), None),
        check_vma=False,
    )
```

profile of v0, /device:TPU:0, one launch (start us, length us, event | category | flops | bytes accessed | tf_op | source)
XLA Modules:
  0.0 114.8 jit_solution(7151662211771608365)
XLA Ops:
  6.5 0.8 iota_compare_fusion
  7.3 0.7 bitcast_convert_fusion
  8.0 0.8 fusion.26
  8.9 1.4 %fusion.36 = (f32[8,2,3]{2,1,0:T(2,128)S(1)}, f32[8,2,3,224]{3,2,1,0:T(4,128)S(1)}) fusion(bf16[8,2,3,128]{3,0,2,1:T(8,128)(2,1)} %bitcast.54, pred[8,224]{1,0:T(8,128)(4,1)S(1)} %iota_compare_fusion, bf16[8,224,256]{2,1,0:T(8,128)(2,1)S(1)} %copy-done), kind=kOutput, calls=%fused_computation.56 | convolution fusion | flops 2784720 | bytes 974784 | tf_op jit(solution)/shard_map/rkgd,rckd->rkgc/dot_general | solution.py:21
  10.3 0.2 fusion.20
  10.5 1.6 %fusion.14 = bf16[8,2,3,128]{3,2,1,0:T(4,128)(2,1)S(1)} fusion(f32[8,2,3,224]{3,2,1,0:T(4,128)S(1)} %get-tuple-element.10, f32[8,2,3]{2,1,0:T(2,128)S(1)} %get-tuple-element.8, f32[8,2,3]{2,1,0:T(2,128)S(1)} %multiply_maximum_fusion, f32[8,2,128]{2,1,0:T(2,128)S(1)} %copy.43, f32[8,2,3]{2,1,0:T(2,128)S(1)} %get-tuple-element.7, bf16[8,224,256]{2,1,0:T(8,128)(2,1)} %param.19), kind=kOutput, calls=%fused_computation.14 | convolution fusion | flops 2803200 | bytes 981568 | tf_op jit(solution)/shard_map/rkgc,rckd->rkgd/dot_general | solution.py:38
  12.1 3.7 %fusion.37 = f32[8,3072]{1,0:T(8,128)} fusion(bf16[8,768]{1,0:T(8,128)(2,1)S(1)} %convert_element_type.60, bf16[768,3072]{1,0:T(8,128)(2,1)} %param.21), kind=kOutput, calls=%fused_computation.57 | convolution fusion | flops 37748736 | bytes 4829184 | tf_op jit(solution)/shard_map/dot_general | solution.py:65
  15.8 0.8 eq.42
  16.7 0.2 select_reduce_fusion
  16.9 36.0 %all-reduce.2.cloned.1.call-done = f32[8,3072]{1,0:T(8,128)} async-done(((f32[8,3072]{1,0:T(8,128)}), f32[8,3072]{1,0:T(8,128)}) %all-reduce.2.cloned.1.call-update) | async-done | bytes 98320 | tf_op jit(solution)/shard_map/psum | solution.py:66
  53.0 1.0 fusion.23
  54.0 0.8 fusion.25
  54.8 0.3 convolution_convert_fusion
  55.1 0.8 broadcast_in_dim.19
  55.9 4.4 %all-to-all-start = ((bf16[16,2,3072]{2,1,0:T(2,128)(2,1)}), bf16[16,2,3072]{2,1,0:T(2,128)(2,1)S(1)}, u32[]{:S(2)}, u32[]{:S(2)}) async-start(bf16[16,2,3072]{2,1,0:T(2,128)(2,1)} %bitcast.6), calls=%async_computation | async-start | bytes 393216 | tf_op jit(solution)/shard_map/all_to_all | solution.py:98
  60.4 8.1 %all-to-all-done = bf16[16,2,3072]{2,1,0:T(2,128)(2,1)S(1)} async-done(((bf16[16,2,3072]{2,1,0:T(2,128)(2,1)}), bf16[16,2,3072]{2,1,0:T(2,128)(2,1)S(1)}, u32[]{:S(2)}, u32[]{:S(2)}) %all-to-all-start) | async-done | bytes 196640 | tf_op jit(solution)/shard_map/all_to_all | solution.py:98
  68.5 6.8 %fusion.4 = f32[32,2048]{1,0:T(8,128)S(1)} fusion(bf16[32,3072]{1,0:T(8,128)(2,1)S(1)} %reshape.105, bf16[1,3072,2048]{2,1,0:T(8,128)(2,1)} %param.25), kind=kOutput, calls=%fused_computation.4 | convolution fusion | flops 402653184 | bytes 13041664 | tf_op jit(solution)/shard_map/dot_general | solution.py:101
  75.4 6.8 %fusion.10 = bf16[32,2048]{1,0:T(8,128)(2,1)S(1)} fusion(bf16[32,3072]{1,0:T(8,128)(2,1)S(1)} %reshape.105, bf16[1,3072,2048]{2,1,0:T(8,128)(2,1)} %param.26, f32[32,2048]{1,0:T(8,128)S(1)} %fusion.4), kind=kOutput, calls=%fused_computation.10 | convolution fusion | flops 403046400 | bytes 13172736 | tf_op jit(solution)/shard_map/dot_general | solution.py:102
  82.4 6.8 %fusion = f32[16,2,3072]{2,0,1:T(8,128)S(1)} fusion(bf16[1,2048,3072]{2,1,0:T(8,128)(2,1)} %param.27, bf16[16,2,2048]{2,1,0:T(2,128)(2,1)S(1)} %dot_general.40), kind=kOutput, calls=%fused_computation | convolution fusion | flops 402653184 | bytes 13107200 | tf_op jit(solution)/shard_map/dot_general | solution.py:104
  89.2 1.1 copy.45
  90.2 3.8 %all-to-all-start.1 = ((f32[16,2,3072]{2,1,0:T(2,128)}), f32[16,2,3072]{2,1,0:T(2,128)S(1)}, u32[]{:S(2)}, u32[]{:S(2)}) async-start(f32[16,2,3072]{2,1,0:T(2,128)} %copy.45), calls=%async_computation.1 | async-start | bytes 786432 | tf_op jit(solution)/shard_map/all_to_all | solution.py:106
  94.3 0.2 fusion.32
  94.6 12.3 %all-to-all-done.1 = f32[16,2,3072]{2,1,0:T(2,128)S(1)} async-done(((f32[16,2,3072]{2,1,0:T(2,128)}), f32[16,2,3072]{2,1,0:T(2,128)S(1)}, u32[]{:S(2)}, u32[]{:S(2)}) %all-to-all-start.1) | async-done | bytes 393248 | tf_op jit(solution)/shard_map/all_to_all | solution.py:106
  107.2 0.8 fusion.6
  (29 shorter events, 1.1 us)
Async XLA Ops:
  6.5 2.3 %copy-start = (bf16[8,224,256]{2,1,0:T(8,128)(2,1)S(1)}, bf16[8,224,256]{2,1,0:T(8,128)(2,1)}, u32[]{:S(2)}) copy-start(bf16[8,224,256]{2,1,0:T(8,128)(2,1)} %param.18) | copy-start | bytes 2752516
  6.5 46.4 %all-reduce.2.cloned.1.call-start = ((), (), s32[]{:S(2)}) async-start(), calls=%async_computation.2 | async-start | bytes 196608 | tf_op jit(solution)/shard_map/psum | solution.py:66
  55.9 12.5 %all-to-all-start = ((bf16[16,2,3072]{2,1,0:T(2,128)(2,1)}), bf16[16,2,3072]{2,1,0:T(2,128)(2,1)S(1)}, u32[]{:S(2)}, u32[]{:S(2)}) async-start(bf16[16,2,3072]{2,1,0:T(2,128)(2,1)} %bitcast.6), calls=%async_computation | async-start | bytes 393216 | tf_op jit(solution)/shard_map/all_to_all | solution.py:98
  82.2 11.9 %copy-start.1 = (s32[2,2]{1,0:T(2,128)S(1)}, s32[2,2]{1,0:T(2,128)}, u32[]{:S(2)}) copy-start(s32[2,2]{1,0:T(2,128)} %param.24) | copy-start | bytes 52
  82.2 11.9 %copy-start.2 = (bf16[3072,4]{0,1:T(4,128)(2,1)S(1)}, bf16[3072,4]{0,1:T(4,128)(2,1)}, u32[]{:S(2)}) copy-start(bf16[3072,4]{0,1:T(4,128)(2,1)} %param.23) | copy-start | bytes 73732
  90.2 16.7 %all-to-all-start.1 = ((f32[16,2,3072]{2,1,0:T(2,128)}), f32[16,2,3072]{2,1,0:T(2,128)S(1)}, u32[]{:S(2)}, u32[]{:S(2)}) async-start(f32[16,2,3072]{2,1,0:T(2,128)} %copy.45), calls=%async_computation.1 | async-start | bytes 786432 | tf_op jit(solution)/shard_map/all_to_all | solution.py:106
Sparse Core Ops, SparseCore 0:
  16.0 36.9 all-reduce.1
where the time goes:
time: 116 us; the launch traced here: 115 us
  waiting for transfers between devices  56.5 us (49%)
  matrix products  29.2 us (25%)
  between operations  13.6 us (12%)
  starting transfers between devices  8.23 us (7%)
  other arithmetic  4.24 us (4%)
  local copies, waits for them, and re-layouts  3.12 us (3%)
    psum x1, waiting for transfers between devices, local(): summed = lax.psum(partial_value, 'tp')  36 us
    all_to_all x1, waiting for transfers between devices, local(): lax.all_to_all(shares, ('node', 'tp'), split_axis=0, concat_axis=0, tiled...  12.3 us
    all_to_all x1, waiting for transfers between devices, local(): lax.all_to_all(outgoing, ('node', 'tp'), split_axis=0, concat_axis=0, til...  8.06 us
    dot_general x1, matrix products, local(): jnp.dot(flattened, up_weight[0], preferred_element_type=jnp.float32)  6.85 us
    dot_general x1, matrix products, local(): jnp.dot(flattened, gate_weight[0], preferred_element_type=jnp.float32)  6.84 us
    dot_general x1, matrix products, local(): jnp.dot(hidden_units, down_weight[0], preferred_element_type=jnp.float32)  6.84 us
    all_to_all x1, starting transfers between devices, local(): lax.all_to_all(outgoing, ('node', 'tp'), split_axis=0, concat_axis=0, til...  4.38 us
    all_to_all x1, starting transfers between devices, local(): lax.all_to_all(shares, ('node', 'tp'), split_axis=0, concat_axis=0, tiled...  3.84 us
  transfers between devices with their start and end apart: 3, of which 3 were waited for; matrix products, arithmetic and copies ran while one was open for 1% of the time, Pallas kernels for 0%

commit v1 on v0

v1 whole, which is shorter than its diff:
```python
import functools
import math

import jax
import jax.numpy as jnp
from jax import lax
from jax.experimental import pallas as pl
from jax.experimental.pallas import tpu as pltpu
from jax.sharding import PartitionSpec as P

HD = 128
LANES = 128
SUB = 8
WIDE = SUB * LANES
MESH = pl.DeviceIdType.MESH
F32 = jnp.float32
BF16 = jnp.bfloat16


def repeat(lo, hi, body):
    if hi - lo <= 16:
        for at in range(lo, hi):
            body(at)
    else:

        def step(at, carry):
            body(at)
            return carry

        lax.fori_loop(lo, hi, step, 0)


def kernel(
    nodes, tps, experts,
    lengths, ids, hidden_in, queries, new_keys, new_values, keys, values,
    out_w, gain, router, gate_w, up_w, down_w,
    out,
    hidden_v, q_v, nk_v, nv_v, k_v, v_v, ow_v, gain_v, router_v, gate_v, up_v, down_v,
    hid_pack, t1, full1, send1, recv1, mid_v, send2, recv2, unpack, lhs, units, lg, t3, send3, recv3,
    local_sem, ow_sem, gate_sem, up_sem, down_sem,
    s1_sem, r1_sem, s2_sem, r2_sem, s3_sem, r3_sem,
):
    count = nodes * tps
    my_node, my_tp = lax.axis_index("node"), lax.axis_index("tp")
    me = my_node * tps + my_tp
    rows = hidden_in.shape[0]
    node_rows = queries.shape[0]
    kv_local = new_keys.shape[1] // HD
    group_size = queries.shape[1] // HD // kv_local
    positions = keys.shape[1]
    wides = hidden_in.shape[1] // WIDE
    unit_chunks, _, unit_wide = gate_v.shape
    split = nodes // experts

    def fetch(src, dst, sem):
        copy = pltpu.make_async_copy(src, dst, sem)
        copy.start()
        return copy

    barrier = pltpu.get_barrier_semaphore()

    def greet(d):
        peer = lax.rem(me + d, count)
        pl.semaphore_signal(
            barrier, inc=1, device_id={"node": peer // tps, "tp": lax.rem(peer, tps)}, device_id_type=MESH
        )

    q_copy = fetch(queries, q_v, local_sem.at[0])
    k_copy = fetch(keys, k_v, local_sem.at[1])
    nk_copy = fetch(new_keys, nk_v, local_sem.at[2])
    v_copy = fetch(values, v_v, local_sem.at[3])
    nv_copy = fetch(new_values, nv_v, local_sem.at[4])
    hidden_copy = fetch(hidden_in, hidden_v, local_sem.at[5])
    gain_copy = fetch(gain, gain_v, local_sem.at[6])
    ow_copies = [
        fetch(out_w.at[:, pl.ds(c * WIDE, WIDE)], ow_v.at[c], ow_sem.at[c]) for c in range(wides)
    ]
    repeat(1, count, greet)
    gate_copies, up_copies = [], []
    for f in range(unit_chunks):
        columns = pl.ds(f * unit_wide, unit_wide)
        gate_copies.append(fetch(gate_w.at[0, :, columns], gate_v.at[f], gate_sem.at[f]))
        up_copies.append(fetch(up_w.at[0, :, columns], up_v.at[f], up_sem.at[f]))
    router_copy = fetch(router, router_v, local_sem.at[7])
    down_copies = [
        fetch(down_w.at[0, :, pl.ds(c * WIDE, WIDE)], down_v.at[c], down_sem.at[c]) for c in range(wides)
    ]

    scaling = 1.0 / math.sqrt(HD)
    row_id = lax.broadcasted_iota(jnp.int32, (node_rows, 1), 0)
    used = jnp.zeros((node_rows, 1), jnp.int32)
    for r in range(node_rows):
        used = jnp.where(row_id == r, lengths[r], used)
    used = jnp.concatenate([used] * group_size, axis=0)
    row_all = jnp.concatenate([row_id] * group_size, axis=0)
    usable = lax.broadcasted_iota(jnp.int32, (group_size * node_rows, positions), 1) < used
    q_copy.wait()
    q_all = q_v[...].astype(F32)
    k_copy.wait()
    nk_copy.wait()
    nk_all = nk_v[...].astype(F32)
    probs, own_probs = [], []
    for k in range(kv_local):
        heads = [
            q_all[:, (k * group_size + g) * HD:(k * group_size + g + 1) * HD] for g in range(group_size)
        ]
        stacked = jnp.concatenate(heads, axis=0)
        stacked16 = stacked.astype(BF16)
        scores = jnp.zeros((group_size * node_rows, positions), F32)
        for r in range(node_rows):
            one = lax.dot_general(
                stacked16, k_v[r, :, k * HD:(k + 1) * HD], (((1,), (1,)), ((), ())), preferred_element_type=F32
            )
            scores = jnp.where(row_all == r, one, scores)
        scores = jnp.where(usable, scores * scaling, -jnp.inf)
        own_key = jnp.concatenate([nk_all[:, k * HD:(k + 1) * HD]] * group_size, axis=0)
        own_score = jnp.sum(stacked * own_key, axis=1, keepdims=True) * scaling
        highest = jnp.maximum(jnp.max(scores, axis=1, keepdims=True), own_score)
        weights = jnp.exp(scores - highest)
        own_weight = jnp.exp(own_score - highest)
        denominator = jnp.sum(weights, axis=1, keepdims=True) + own_weight
        probs.append((weights / denominator).astype(BF16))
        own_probs.append((own_weight / denominator).astype(BF16).astype(F32))
    v_copy.wait()
    nv_copy.wait()
    nv_all = nv_v[...].astype(F32)
    attended = []
    for k in range(kv_local):
        mixture = jnp.zeros((group_size * node_rows, HD), F32)
        for r in range(node_rows):
            one = jnp.dot(probs[k], v_v[r, :, k * HD:(k + 1) * HD], preferred_element_type=F32)
            mixture = jnp.where(row_all == r, one, mixture)
        own_value = jnp.concatenate([nv_all[:, k * HD:(k + 1) * HD]] * group_size, axis=0)
        mixture = mixture + own_probs[k] * own_value
        for g in range(group_size):
            attended.append(mixture[g * node_rows:(g + 1) * node_rows])
    attended = jnp.concatenate(attended, axis=1).astype(BF16)

    hidden_copy.wait()
    hidden_all = hidden_v[...].astype(F32)
    for c in range(wides):
        for i in range(rows):
            for q in range(SUB):
                at = c * WIDE + q * LANES
                hid_pack[c, i * SUB + q:i * SUB + q + 1, :] = hidden_all[i:i + 1, at:at + LANES]

    pl.semaphore_wait(barrier, count - 1)

    def along_tp(d, c):
        peer = lax.rem(my_tp + d, tps)
        return pltpu.make_async_remote_copy(
            src_ref=send1.at[peer, c], dst_ref=recv1.at[my_tp, c],
            send_sem=s1_sem.at[d, c], recv_sem=r1_sem.at[my_tp, c],
            device_id={"tp": peer}, device_id_type=MESH,
        )

    def from_tp(d, c):
        peer = lax.rem(my_tp + d, tps)
        return pltpu.make_async_remote_copy(
            src_ref=send1.at[peer, c], dst_ref=recv1.at[peer, c],
            send_sem=s1_sem.at[d, c], recv_sem=r1_sem.at[peer, c],
            device_id={"tp": peer}, device_id_type=MESH,
        )

    for c in range(wides):
        ow_copies[c].wait()
        partial = jnp.dot(attended, ow_v[c], preferred_element_type=F32)
        for q in range(SUB):
            t1[c, q * node_rows:(q + 1) * node_rows, :] = partial[:, q * LANES:(q + 1) * LANES]
        for j in range(tps):
            block = jnp.concatenate(
                [t1[c, pl.ds(j * rows + i, SUB, stride=node_rows), :] for i in range(rows)], axis=0
            )
            full1[j, c] = block
            send1[j, c] = block.astype(BF16)
        for d in range(1, tps):
            along_tp(d, c).start()

    gain_copy.wait()
    squares = [jnp.zeros((SUB, LANES), F32) for _ in range(rows)]
    for c in range(wides):
        total = full1[my_tp, c]
        for d in range(1, tps):
            from_tp(d, c).wait_recv()
            total = total + recv1[lax.rem(my_tp + d, tps), c].astype(F32)
        middle = (hid_pack[c] + total).astype(BF16).astype(F32)
        mid_v[c] = middle
        for i in range(rows):
            piece = middle[i * SUB:(i + 1) * SUB]
            squares[i] = squares[i] + piece * piece
    scales = []
    for i in range(rows):
        mean = jnp.sum(jnp.sum(squares[i], axis=1, keepdims=True), axis=0, keepdims=True) / (wides * WIDE)
        scales.append(lax.rsqrt(mean + 1e-05))
    for c in range(wides):
        pieces = [mid_v[c, i * SUB:(i + 1) * SUB, :] * scales[i] * gain_v[c] for i in range(rows)]
        normed = jnp.concatenate(pieces, axis=0).astype(BF16)
        send2[c] = normed
        recv2[me, c] = normed

    def spread(d, slot):
        peer = lax.rem(me + d, count)
        return pltpu.make_async_remote_copy(
            src_ref=send2, dst_ref=recv2.at[slot],
            send_sem=s2_sem.at[d], recv_sem=r2_sem.at[slot],
            device_id={"node": peer // tps, "tp": lax.rem(peer, tps)}, device_id_type=MESH,
        )

    repeat(1, count, lambda d: spread(d, me).start())
    repeat(1, count, lambda d: spread(d, lax.rem(me + d, count)).wait_recv())

    for c in range(wides):
        for n in range(nodes):
            for j in range(tps):
                unpack[n, c, j * rows * SUB:(j + 1) * rows * SUB, :] = recv2[n * tps + j, c].astype(F32)
        for q in range(SUB):
            column = jnp.concatenate(
                [unpack[n, c, pl.ds(q, node_rows, stride=SUB), :] for n in range(nodes)], axis=0
            )
            at = c * WIDE + q * LANES
            lhs[:, at:at + LANES] = column.astype(BF16)

    for f in range(unit_chunks):
        gate_copies[f].wait()
        gate = jnp.dot(lhs[...], gate_v[f], preferred_element_type=F32)
        up_copies[f].wait()
        up = jnp.dot(lhs[...], up_v[f], preferred_element_type=F32)
        units[:, f * unit_wide:(f + 1) * unit_wide] = (gate / (1.0 + jnp.exp(-gate)) * up).astype(BF16)

    def give(d, slot, c):
        peer = lax.rem(me + d, count)
        return pltpu.make_async_remote_copy(
            src_ref=send3.at[peer, c], dst_ref=recv3.at[slot, c],
            send_sem=s3_sem.at[d, c], recv_sem=r3_sem.at[slot, c],
            device_id={"node": peer // tps, "tp": lax.rem(peer, tps)}, device_id_type=MESH,
        )

    for c in range(wides):
        down_copies[c].wait()
        share = jnp.dot(units[...], down_v[c], preferred_element_type=F32)
        for n in range(nodes):
            for q in range(SUB):
                t3[c, n, q * node_rows:(q + 1) * node_rows, :] = share[
                    n * node_rows:(n + 1) * node_rows, q * LANES:(q + 1) * LANES
                ]
            for j in range(tps):
                block = jnp.concatenate(
                    [t3[c, n, pl.ds(j * rows + i, SUB, stride=node_rows), :] for i in range(rows)], axis=0
                )
                send3[n * tps + j, c] = block.astype(BF16)
        repeat(1, count, lambda d: give(d, me, c).start())
        recv3[me, c] = send3[me, c]

    router_copy.wait()
    lg[...] = jnp.dot(lhs[...], router_v[...], preferred_element_type=F32)
    mixing = []
    for i in range(rows):
        logit = lg[pl.ds(me * rows + i, 1), :]
        lane = lax.broadcasted_iota(jnp.int32, logit.shape, 1)
        picked = [
            jnp.sum(jnp.where(lane == ids[i, k], logit, 0.0), axis=1, keepdims=True) for k in range(2)
        ]
        gates = [1.0 / (1.0 + jnp.exp(picked[1 - k] - picked[k])) for k in range(2)]
        mixing.append([
            sum(jnp.where(ids[i, k] == e, gates[k], 0.0) for k in range(2)) for e in range(experts)
        ])

    for c in range(wides):
        repeat(1, count, lambda d: give(d, lax.rem(me + d, count), c).wait_recv())
        pieces = []
        sums = [
            functools.reduce(
                lambda a, b: a + b,
                [recv3[s, c].astype(F32) for s in range(e * split * tps, (e + 1) * split * tps)],
            )
            for e in range(experts)
        ]
        for i in range(rows):
            piece = jnp.zeros((SUB, LANES), F32)
            for e in range(experts):
                piece = piece + mixing[i][e] * sums[e][i * SUB:(i + 1) * SUB]
            pieces.append(mid_v[c, i * SUB:(i + 1) * SUB, :] + piece)
        out[c] = jnp.concatenate(pieces, axis=0).astype(BF16)

    for c in range(wides):
        for d in range(1, tps):
            along_tp(d, c).wait_send()
        repeat(1, count, lambda d: give(d, me, c).wait_send())
    repeat(1, count, lambda d: spread(d, me).wait_send())


def local(
    nodes, tps,
    hidden_in, queries, new_keys, new_values, key_cache, value_cache, lengths,
    out_weight, norm_gain, router, expert_ids, gate_weight, up_weight, down_weight,
):
    rows, width = hidden_in.shape
    count = nodes * tps
    node_rows = queries.shape[0]
    wides = width // WIDE
    experts = router.shape[1]
    units = gate_weight.shape[2]
    unit_wide = min(units, 512)
    unit_chunks = units // unit_wide
    total_rows = nodes * node_rows
    depth = out_weight.shape[0]
    packed = (wides, rows * SUB, LANES)
    anywhere = pl.BlockSpec(memory_space=pl.ANY)
    smem = pl.BlockSpec(memory_space=pltpu.SMEM)
    vmem = pltpu.VMEM
    dma = pltpu.SemaphoreType.DMA
    result = pl.pallas_call(
        functools.partial(kernel, nodes, tps, experts),
        out_shape=jax.ShapeDtypeStruct(packed, BF16),
        in_specs=[smem, smem] + [anywhere] * 12,
        out_specs=pl.BlockSpec(memory_space=pltpu.VMEM),
        scratch_shapes=[
            vmem(hidden_in.shape, BF16),
            vmem(queries.shape, BF16),
            vmem(new_keys.shape, BF16),
            vmem(new_values.shape, BF16),
            vmem(key_cache.shape, BF16),
            vmem(value_cache.shape, BF16),
            vmem((wides, depth, WIDE), BF16),
            vmem((wides, SUB, LANES), F32),
            vmem(router.shape, BF16),
            vmem((unit_chunks, width, unit_wide), BF16),
            vmem((unit_chunks, width, unit_wide), BF16),
            vmem((wides, units, WIDE), BF16),
            vmem(packed, F32),
            vmem((wides, SUB * node_rows, LANES), F32),
            vmem((tps,) + packed, F32),
            vmem((tps,) + packed, BF16),
            vmem((tps,) + packed, BF16),
            vmem(packed, F32),
            vmem(packed, BF16),
            vmem((count,) + packed, BF16),
            vmem((nodes, wides, tps * rows * SUB, LANES), F32),
            vmem((total_rows, width), BF16),
            vmem((total_rows, units), BF16),
            vmem((total_rows, experts), F32),
            vmem((wides, nodes, SUB * node_rows, LANES), F32),
            vmem((count,) + packed, BF16),
            vmem((count,) + packed, BF16),
            dma((8,)),
            dma((wides,)),
            dma((unit_chunks,)),
            dma((unit_chunks,)),
            dma((wides,)),
            dma((tps, wides)),
            dma((tps, wides)),
            dma((count,)),
            dma((count,)),
            dma((count, wides)),
            dma((count, wides)),
        ],
        compiler_params=pltpu.CompilerParams(
            collective_id=0, has_side_effects=True, vmem_limit_bytes=60 * 1024 * 1024
        ),
    )(
        lengths, expert_ids, hidden_in, queries, new_keys, new_values, key_cache, value_cache,
        out_weight, norm_gain.reshape(wides, SUB, LANES), router, gate_weight, up_weight, down_weight,
    )
    split_rows = result.reshape(wides, rows, SUB, LANES)
    return jnp.transpose(split_rows, (1, 0, 2, 3)).reshape(rows, width)


def solution(mesh):
    placed = (
        P(("group", "node", "tp"), None),
        P(("group", "node"), "tp"),
        P(("group", "node"), "tp"),
        P(("group", "node"), "tp"),
        P(("group", "node"), None, "tp"),
        P(("group", "node"), None, "tp"),
        P(("group", "node")),
        P("tp", None),
        P(),
        P(),
        P(("group", "node", "tp"), None),
        P("node", None, "tp"),
        P("node", None, "tp"),
        P("node", "tp", None),
    )
    return jax.shard_map(
        functools.partial(local, mesh.shape["node"], mesh.shape["tp"]),
        mesh=mesh,
        in_specs=placed,
        out_specs=P(("group", "node", "tp"), None),
        check_vma=False,
    )
```

time: 116 us -> 35.3 us (0.30)
  waiting for transfers between devices: 56.5 us -> 0 us
  Pallas kernels: 0 us -> 31.7 us
  matrix products: 29.2 us -> 0 us
  between operations: 13.6 us -> 0.01 us
  starting transfers between devices: 8.23 us -> 0 us
  other arithmetic: 4.24 us -> 0 us
    psum x1 -> x0, waiting for transfers between devices: 36 us -> none  [local(): summed = lax.psum(partial_value, 'tp')]
    pallas_call x0 -> x1, Pallas kernels: none -> 31.7 us  [local(): pl.pallas_call(functools.partial(kernel, nodes, tps, experts), out_shape=...]
    dot_general x10 -> x0, matrix products: 29.2 us -> none  [the longest x1 6.85 us: local(): jnp.dot(flattened, up_weight[0], preferred_element_type=jnp.float32)]
    all_to_all x2 -> x0, waiting for transfers between devices: 20.4 us -> none  [the longest x1 12.3 us: local(): lax.all_to_all(shares, ('node', 'tp'), split_axis=0, concat_axis=0, tiled...]
    all_to_all x2 -> x0, starting transfers between devices: 8.23 us -> none  [the longest x1 4.38 us: local(): lax.all_to_all(outgoing, ('node', 'tp'), split_axis=0, concat_axis=0, til...]
    unnamed x6 -> x3, local copies, waits for them, and re-layouts: 0.02 us -> 3.27 us
    reduce_sum x6 -> x0, other arithmetic: 1.77 us -> none  [the longest x1 1.04 us: local(): jnp.mean(widened * widened, axis=-1, keepdims=True) + 1e-05]
    convert_element_type x4 -> x0, other arithmetic: 1.58 us -> none  [the longest x1 0.79 us: local(): normed = (widened * scale_rms * norm_gain).astype(jnp.bfloat16)]
  transfers between devices with their start and end apart: 3 -> 0, of which waited for: 3 -> 0; matrix products, arithmetic and copies ran while one was open for 1% -> 0% of each run, Pallas kernels for 0% -> 0%
where the time goes in v1:
time: 35.3 us; the launch traced here: 35 us
  Pallas kernels  31.7 us (90%)
  local copies, waits for them, and re-layouts  3.27 us (9%)
    pallas_call x1, Pallas kernels, local(): pl.pallas_call(functools.partial(kernel, nodes, tps, experts), out_shape=...  31.7 us
    unnamed x3, local copies, waits for them, and re-layouts  3.27 us

profile of v1, /device:TPU:0, one launch (start us, length us, event | category | flops | bytes accessed | tf_op | source)
XLA Modules:
  0.0 35.0 jit_solution(15689150762478070853)
XLA Ops:
  0.0 2.0 %copy.15.router = bf16[3072,4]{1,0:T(8,128)(2,1)} copy(bf16[3072,4]{0,1:T(4,128)(2,1)} %param.23) | data formatting | bytes 49152 | tf_op args[9]
  2.0 31.7 %shard_map.136 = bf16[3,16,128]{2,1,0:T(8,128)(2,1)} custom-call(s32[8]{0:T(128)} %lengths.1, s32[2,2]{1,0:T(2,128)} %ids.1, bf16[2,3072]{1,0:T(2,128)(2,1)} %hidden_in.1, bf16[8,768]{1,0:T(8,128)(2,1)} %queries.1, bf16[8,256]{1,0:T(8,128)(2,1)} %new_keys.1, bf16[8,256]{1,0:T(8,128)(2,1)} %new_values.1, bf16[8,224,256]{2,1,0:T(8,128)(2,1)} %keys.1, ...), custom_call_target="tpu_custom_call" | custom-call | tf_op jit(solution)/shard_map/pallas_call | solution.py:312
  33.7 0.7 %copy_bitcast_fusion.1 = bf16[1,2,24,128]{3,2,1,0:T(8,128)(2,1)S(1)} fusion(bf16[3,16,128]{2,1,0:T(8,128)(2,1)} %shard_map.136), kind=kLoop, calls=%fused_computation.1 | loop fusion | bytes 24576
  34.4 0.6 %copy.20 = bf16[1,2,24,128]{3,1,2,0:T(2,128)(2,1)} copy(bf16[1,2,24,128]{3,2,1,0:T(8,128)(2,1)S(1)} %copy_bitcast_fusion.1) | data formatting | bytes 24576

commit v2 on v1

--- a/solution.py
+++ b/solution.py
@@ -36,7 +36,7 @@
     out_w, gain, router, gate_w, up_w, down_w,
     out,
     hidden_v, q_v, nk_v, nv_v, k_v, v_v, ow_v, gain_v, router_v, gate_v, up_v, down_v,
-    hid_pack, t1, full1, send1, recv1, mid_v, send2, recv2, unpack, lhs, units, lg, t3, send3, recv3,
+    hid_pack, t1, full1, send1, recv1, mid_v, send2, recv2, unpack, lhs, units, lg, t3, send3, recv3, flat,
     local_sem, ow_sem, gate_sem, up_sem, down_sem,
     s1_sem, r1_sem, s2_sem, r2_sem, s3_sem, r3_sem,
 ):
@@ -65,6 +65,7 @@
             barrier, inc=1, device_id={"node": peer // tps, "tp": lax.rem(peer, tps)}, device_id_type=MESH
         )
 
+    repeat(1, count, greet)
     q_copy = fetch(queries, q_v, local_sem.at[0])
     k_copy = fetch(keys, k_v, local_sem.at[1])
     nk_copy = fetch(new_keys, nk_v, local_sem.at[2])
@@ -75,16 +76,14 @@
     ow_copies = [
         fetch(out_w.at[:, pl.ds(c * WIDE, WIDE)], ow_v.at[c], ow_sem.at[c]) for c in range(wides)
     ]
-    repeat(1, count, greet)
-    gate_copies, up_copies = [], []
-    for f in range(unit_chunks):
-        columns = pl.ds(f * unit_wide, unit_wide)
-        gate_copies.append(fetch(gate_w.at[0, :, columns], gate_v.at[f], gate_sem.at[f]))
-        up_copies.append(fetch(up_w.at[0, :, columns], up_v.at[f], up_sem.at[f]))
-    router_copy = fetch(router, router_v, local_sem.at[7])
-    down_copies = [
-        fetch(down_w.at[0, :, pl.ds(c * WIDE, WIDE)], down_v.at[c], down_sem.at[c]) for c in range(wides)
-    ]
+    gate_copies, up_copies, down_copies = [], [], []
+
+    def fetch_units(lo, hi):
+        for f in range(lo, hi):
+            columns = pl.ds(f * unit_wide, unit_wide)
+            gate_copies.append(fetch(gate_w.at[0, :, columns], gate_v.at[f], gate_sem.at[f]))
+            up_copies.append(fetch(up_w.at[0, :, columns], up_v.at[f], up_sem.at[f]))
+
 
     scaling = 1.0 / math.sqrt(HD)
     row_id = lax.broadcasted_iota(jnp.int32, (node_rows, 1), 0)
@@ -97,6 +96,7 @@
     q_copy.wait()
     q_all = q_v[...].astype(F32)
     k_copy.wait()
+    fetch_units(0, 1)
     nk_copy.wait()
     nk_all = nk_v[...].astype(F32)
     probs, own_probs = [], []
@@ -123,6 +123,7 @@
         own_probs.append((own_weight / denominator).astype(BF16).astype(F32))
     v_copy.wait()
     nv_copy.wait()
+    fetch_units(1, unit_chunks)
     nv_all = nv_v[...].astype(F32)
     attended = []
     for k in range(kv_local):
@@ -176,6 +177,11 @@
         for d in range(1, tps):
             along_tp(d, c).start()
 
+    router_copy = fetch(router, router_v, local_sem.at[7])
+    for c in range(wides):
+        down_copies.append(
+            fetch(down_w.at[0, :, pl.ds(c * WIDE, WIDE)], down_v.at[c], down_sem.at[c])
+        )
     gain_copy.wait()
     squares = [jnp.zeros((SUB, LANES), F32) for _ in range(rows)]
     for c in range(wides):
@@ -252,7 +258,9 @@
         recv3[me, c] = send3[me, c]
 
     router_copy.wait()
-    lg[...] = jnp.dot(lhs[...], router_v[...], preferred_element_type=F32)
+    lg[...] = lax.dot_general(
+        lhs[...], router_v[...], (((1,), (1,)), ((), ())), preferred_element_type=F32
+    )
     mixing = []
     for i in range(rows):
         logit = lg[pl.ds(me * rows + i, 1), :]
@@ -267,7 +275,6 @@
 
     for c in range(wides):
         repeat(1, count, lambda d: give(d, lax.rem(me + d, count), c).wait_recv())
-        pieces = []
         sums = [
             functools.reduce(
                 lambda a, b: a + b,
@@ -279,8 +286,11 @@
             piece = jnp.zeros((SUB, LANES), F32)
             for e in range(experts):
                 piece = piece + mixing[i][e] * sums[e][i * SUB:(i + 1) * SUB]
-            pieces.append(mid_v[c, i * SUB:(i + 1) * SUB, :] + piece)
-        out[c] = jnp.concatenate(pieces, axis=0).astype(BF16)
+            piece = mid_v[c, i * SUB:(i + 1) * SUB, :] + piece
+            for q in range(SUB):
+                at = c * WIDE + q * LANES
+                flat[i:i + 1, at:at + LANES] = piece[q:q + 1]
+    out[...] = flat[...].astype(BF16)
 
     for c in range(wides):
         for d in range(1, tps):
@@ -309,9 +319,9 @@
     smem = pl.BlockSpec(memory_space=pltpu.SMEM)
     vmem = pltpu.VMEM
     dma = pltpu.SemaphoreType.DMA
-    result = pl.pallas_call(
+    return pl.pallas_call(
         functools.partial(kernel, nodes, tps, experts),
-        out_shape=jax.ShapeDtypeStruct(packed, BF16),
+        out_shape=jax.ShapeDtypeStruct((rows, width), BF16),
         in_specs=[smem, smem] + [anywhere] * 12,
         out_specs=pl.BlockSpec(memory_space=pltpu.VMEM),
         scratch_shapes=[
@@ -323,7 +333,7 @@
             vmem(value_cache.shape, BF16),
             vmem((wides, depth, WIDE), BF16),
             vmem((wides, SUB, LANES), F32),
-            vmem(router.shape, BF16),
+            vmem(router.shape[::-1], BF16),
             vmem((unit_chunks, width, unit_wide), BF16),
             vmem((unit_chunks, width, unit_wide), BF16),
             vmem((wides, units, WIDE), BF16),
@@ -342,6 +352,7 @@
             vmem((wides, nodes, SUB * node_rows, LANES), F32),
             vmem((count,) + packed, BF16),
             vmem((count,) + packed, BF16),
+            vmem((rows, width), F32),
             dma((8,)),
             dma((wides,)),
             dma((unit_chunks,)),
@@ -359,10 +370,8 @@
         ),
     )(
         lengths, expert_ids, hidden_in, queries, new_keys, new_values, key_cache, value_cache,
-        out_weight, norm_gain.reshape(wides, SUB, LANES), router, gate_weight, up_weight, down_weight,
+        out_weight, norm_gain.reshape(wides, SUB, LANES), router.T, gate_weight, up_weight, down_weight,
     )
-    split_rows = result.reshape(wides, rows, SUB, LANES)
-    return jnp.transpose(split_rows, (1, 0, 2, 3)).reshape(rows, width)
 
 
 def solution(mesh):

time: 35.3 us -> 33.4 us (0.946)
  local copies, waits for them, and re-layouts: 3.27 us -> 1.32 us
    unnamed x3 -> x1, local copies, waits for them, and re-layouts: 3.27 us -> 1.32 us
where the time goes in v2:
time: 33.4 us; the launch traced here: 33.1 us
  Pallas kernels  31.8 us (95%)
  local copies, waits for them, and re-layouts  1.32 us (4%)
    pallas_call x1, Pallas kernels, local(): pl.pallas_call(functools.partial(kernel, nodes, tps, experts), out_shape=...  31.8 us
    unnamed x1, local copies, waits for them, and re-layouts  1.32 us

profile of v2, /device:TPU:0, one launch (start us, length us, event | category | flops | bytes accessed | tf_op | source)
XLA Modules:
  0.0 33.1 jit_solution(6625051548762537180)
XLA Ops:
  0.0 31.8 %shard_map.136 = bf16[2,3072]{1,0:T(2,128)(2,1)} custom-call(s32[8]{0:T(128)} %lengths.1, s32[2,2]{1,0:T(2,128)} %ids.1, bf16[2,3072]{1,0:T(2,128)(2,1)} %hidden_in.1, bf16[8,768]{1,0:T(8,128)(2,1)} %queries.1, bf16[8,256]{1,0:T(8,128)(2,1)} %new_keys.1, bf16[8,256]{1,0:T(8,128)(2,1)} %new_values.1, bf16[8,224,256]{2,1,0:T(8,128)(2,1)} %keys.1, ...), custom_call_target="tpu_custom_call" | custom-call | tf_op jit(solution)/shard_map/pallas_call | solution.py:322
  31.8 1.3 %copy.16 = bf16[2,3072]{1,0:T(2,128)(2,1)} copy(bf16[2,3072]{1,0:T(2,128)(2,1)} %shard_map.136) | data formatting | bytes 24576

commit v3 on v2

--- a/solution.py
+++ b/solution.py
@@ -204,16 +204,41 @@
         send2[c] = normed
         recv2[me, c] = normed
 
-    def spread(d, slot):
-        peer = lax.rem(me + d, count)
+    pairs = count // 2
+    core = lax.rem(my_node, 2)
+    partner = {"node": my_node + 1 - 2 * core, "tp": my_tp}
+    my_pair = my_node // 2 * tps + my_tp
+
+    def device_of(pair, of_core):
+        return pair // tps * 2 + of_core, lax.rem(pair, tps)
+
+    def slot_of(pair, of_core):
+        node, at = device_of(pair, of_core)
+        return node * tps + at
+
+    def spread(d):
+        node, at = device_of(lax.rem(my_pair + d, pairs), core)
         return pltpu.make_async_remote_copy(
-            src_ref=send2, dst_ref=recv2.at[slot],
-            send_sem=s2_sem.at[d], recv_sem=r2_sem.at[slot],
-            device_id={"node": peer // tps, "tp": lax.rem(peer, tps)}, device_id_type=MESH,
-        )
-
-    repeat(1, count, lambda d: spread(d, me).start())
-    repeat(1, count, lambda d: spread(d, lax.rem(me + d, count)).wait_recv())
+            src_ref=send2, dst_ref=recv2.at[me], send_sem=s2_sem.at[d], recv_sem=r2_sem.at[me],
+            device_id={"node": node, "tp": at}, device_id_type=MESH,
+        )
+
+    def hand(d, of_core):
+        slot = slot_of(lax.rem(my_pair + pairs - d, pairs), of_core)
+        return pltpu.make_async_remote_copy(
+            src_ref=recv2.at[slot], dst_ref=recv2.at[slot],
+            send_sem=s2_sem.at[pairs + d], recv_sem=r2_sem.at[slot],
+            device_id=partner, device_id_type=MESH,
+        )
+
+    def pass_on(d):
+        hand(d, core).wait_recv()
+        hand(d, core).start()
+
+    repeat(1, pairs, lambda d: spread(d).start())
+    hand(0, core).start()
+    repeat(1, pairs, pass_on)
+    repeat(0, pairs, lambda d: hand(d, 1 - core).wait_recv())
 
     for c in range(wides):
         for n in range(nodes):
@@ -296,7 +321,8 @@
         for d in range(1, tps):
             along_tp(d, c).wait_send()
         repeat(1, count, lambda d: give(d, me, c).wait_send())
-    repeat(1, count, lambda d: spread(d, me).wait_send())
+    repeat(1, pairs, lambda d: spread(d).wait_send())
+    repeat(0, pairs, lambda d: hand(d, core).wait_send())
 
 
 def local(

time: 33.4 us -> 33.2 us (level)
  no operation moved by 1% of the time
where the time goes in v3:
time: 33.2 us; the launch traced here: 32.9 us
  Pallas kernels  31.5 us (95%)
  local copies, waits for them, and re-layouts  1.32 us (4%)
    pallas_call x1, Pallas kernels, local(): pl.pallas_call(functools.partial(kernel, nodes, tps, experts), out_shape=...  31.5 us
    unnamed x1, local copies, waits for them, and re-layouts  1.32 us

profile of v3, /device:TPU:0, one launch (start us, length us, event | category | flops | bytes accessed | tf_op | source)
XLA Modules:
  0.0 32.9 jit_solution(8319780910150533569)
XLA Ops:
  0.0 31.5 %shard_map.136 = bf16[2,3072]{1,0:T(2,128)(2,1)} custom-call(s32[8]{0:T(128)} %lengths.1, s32[2,2]{1,0:T(2,128)} %ids.1, bf16[2,3072]{1,0:T(2,128)(2,1)} %hidden_in.1, bf16[8,768]{1,0:T(8,128)(2,1)} %queries.1, bf16[8,256]{1,0:T(8,128)(2,1)} %new_keys.1, bf16[8,256]{1,0:T(8,128)(2,1)} %new_values.1, bf16[8,224,256]{2,1,0:T(8,128)(2,1)} %keys.1, ...), custom_call_target="tpu_custom_call" | custom-call | tf_op jit(solution)/shard_map/pallas_call | solution.py:348
  31.6 1.3 %copy.16 = bf16[2,3072]{1,0:T(2,128)(2,1)} copy(bf16[2,3072]{1,0:T(2,128)(2,1)} %shard_map.136) | data formatting | bytes 24576
